TPU v7x, 32 devices: a whole 2x2x4 slice. The times are simulated.
32 devices in a mesh: slab: 4 (over y, core), hst: 8 (over z, x).
Axes of the slice: x: 2, y: 2, z: 4, core: 2. Of those that a mesh axis runs over, the one named last changes fastest.
Arguments:
- load: bfloat16 [288, 65536], P('slab', 'hst'), may hold values from -6 to 6
- host_rack: int32 [65536], P('hst'), may hold values from 0 to 2047, as said below
- rack_pod: int32 [2048], P('hst'), may hold values from 0 to 15
Outputs:
- host_drift: float32 [288, 65536], P('slab', 'hst')
- rack_drift: float32 [288, 2048], P('slab', 'hst')
- pod_drift: float32 [288, 16], P('slab', 'hst')
Inputs may be any that keep to these rules, and one draw needn't show every extreme that they name: `host_rack`: the hosts s * 8192 to (s + 1) * 8192 - 1 belong to racks among s * 256 to (s + 2) * 256 - 1, counted modulo 2048; racks hold uneven numbers of hosts, some none.
All inputs are finite; a program needn't handle non-finite values.
Results may differ from a plain program's by a relative error of at most 0.0003.
Values may be sent and summed in bfloat16 or wider, within the bound.
A program may use at most 64 MiB of HBM per device.

v0:
```python
import functools
import math

import jax
import jax.numpy as jnp
from jax import lax
from jax.experimental import pallas as pl
from jax.experimental.pallas import tpu as pltpu
from jax.sharding import PartitionSpec as P

SLAB_LEN = 36
POD_DEV = 2
SLABS = 4
PARTS = 8
AHEAD = 5
MESH = pl.DeviceIdType.MESH
EXACT = lax.Precision.HIGHEST
NT = (((1,), (1,)), ((), ()))


def coefficients(target, source, out_rows, rows):
    reach = 2 * SLAB_LEN
    day = SLABS * rows
    t = target * rows + lax.broadcasted_iota(jnp.int32, (out_rows, rows), 0)
    u = source * rows + lax.broadcasted_iota(jnp.int32, (out_rows, rows), 1)
    value = jnp.where(u <= t, 2 * reach + 1, 0)
    for wrap in (-day, 0, day):
        first = jnp.maximum(u + (wrap - reach), 0)
        last = jnp.minimum(u + (wrap + reach), t)
        value = value - jnp.maximum(last - first + 1, 0)
    return value.astype(jnp.float32)


def kernel(
    shards,
    load_hbm,
    rack_hbm,
    pod_hbm,
    host_out,
    rack_out,
    pod_out,
    own,
    near,
    far,
    rack_ref,
    pod_ref,
    local_rack,
    partial,
    spill,
    totals,
    near_totals,
    far_totals,
    pod_terms,
    pod_in,
    pod_sum,
    slab_pods,
    rack_row,
    rack_row_in,
    host_row,
    host_row_in,
    load_sems,
    near_sems,
    far_send,
    far_recv,
    small_send,
    small_recv,
    pod_send,
    pod_recv,
):
    rows, hosts = own.shape
    racks = totals.shape[1]
    width = hosts // PARTS
    d = lax.axis_index("slab")
    h = lax.axis_index("hst")
    odd = lax.rem(d, 2)
    near_d = d + 1 - 2 * odd
    far_d = lax.rem(d + 3 + 2 * odd, SLABS)
    diag_d = lax.rem(d + 2, SLABS)
    window = 4 * SLAB_LEN + 1
    day = SLABS * rows

    barrier = pltpu.get_barrier_semaphore()
    for peer in (near_d, far_d, diag_d):
        pl.semaphore_signal(barrier, inc=1, device_id=(peer, h), device_id_type=MESH)

    @pl.loop(1, shards)
    def _(k):
        peer = lax.rem(h + k, shards)
        pl.semaphore_signal(barrier, inc=1, device_id=(d, peer), device_id_type=MESH)

    loads = [
        pltpu.make_async_copy(rack_hbm, rack_ref, load_sems.at[0]),
        pltpu.make_async_copy(pod_hbm, pod_ref, load_sems.at[1]),
        pltpu.make_async_copy(load_hbm, own, load_sems.at[2]),
    ]
    for copy in loads:
        copy.start()
    pl.semaphore_wait(barrier, SLABS - 1 + shards - 1)

    def far_copy(c):
        cols = pl.ds(pl.multiple_of(c * width, width), width)
        return pltpu.make_async_remote_copy(
            src_ref=load_hbm.at[:, cols],
            dst_ref=far.at[:, cols],
            send_sem=far_send.at[c],
            recv_sem=far_recv.at[c],
            device_id=(far_d, h),
            device_id_type=MESH,
        )

    def small_copy(src, dst, index, device):
        return pltpu.make_async_remote_copy(
            src_ref=src,
            dst_ref=dst,
            send_sem=small_send.at[index],
            recv_sem=small_recv.at[index],
            device_id=device,
            device_id_type=MESH,
        )

    for c in range(AHEAD):
        far_copy(c).start()
    near_copy = pltpu.make_async_remote_copy(
        src_ref=load_hbm,
        dst_ref=near,
        send_sem=near_sems.at[0],
        recv_sem=near_sems.at[1],
        device_id=(near_d, h),
        device_id_type=MESH,
    )
    near_copy.start()
    for copy in loads:
        copy.wait()
    local = rack_ref[...] - h * racks
    local_rack[...] = jnp.where(local < 0, local + racks * shards, local)

    def next_far(c):
        far_copy(c - AHEAD).wait_send()
        far_copy(c).start()

    partial[...] = jnp.zeros_like(partial)
    rack_ids = lax.broadcasted_iota(jnp.int32, (2 * racks, 128), 0)

    @pl.loop(0, PARTS)
    def _(c):
        cols = pl.ds(pl.multiple_of(c * width, width), width)
        member = jnp.concatenate(
            [
                (rack_ids == local_rack[pl.ds(c * (width // 128) + k, 1), :])
                .astype(jnp.float32)
                .astype(jnp.bfloat16)
                for k in range(width // 128)
            ],
            axis=1,
        )
        partial[...] += lax.dot_general(
            own[:, cols], member, NT, preferred_element_type=jnp.float32
        )

    spill_copy = small_copy(
        partial.at[:, pl.ds(racks, racks)], spill, 0, (d, lax.rem(h + 1, shards))
    )
    spill_copy.start()
    next_far(AHEAD)

    k_own = coefficients(d, d, rows, rows)
    k_near = coefficients(d, near_d, rows, rows)
    k_far = coefficients(d, far_d, rows, rows)
    k_diag = coefficients(diag_d, d, 8, rows)
    k_both = jnp.concatenate([k_own, k_diag], 0).astype(jnp.bfloat16)

    @pl.loop(0, PARTS)
    def _(c):
        cols = pl.ds(pl.multiple_of(c * width, width), width)
        both = jnp.dot(k_both, own[:, cols], preferred_element_type=jnp.float32)
        host_out[:, cols] = both[:rows]
        host_row[pl.ds(c, 1), :] = both[rows : rows + 1]

    host_row_copy = small_copy(host_row, host_row_in, 1, (diag_d, h))
    host_row_copy.start()

    spill_copy.wait()
    totals[...] = partial[:, :racks] + spill[...]
    slots = lax.broadcasted_iota(jnp.int32, (8 * shards, 128), 0)
    slot_pod = jnp.where(slots % 8 < POD_DEV, slots // 8 * POD_DEV + slots % 8, -1)
    pod_member = jnp.concatenate(
        [
            (slot_pod == pod_ref[pl.ds(k, 1), :]).astype(jnp.float32)
            for k in range(racks // 128)
        ],
        axis=1,
    )
    pod_terms[...] = lax.dot_general(
        pod_member, totals[...], NT, preferred_element_type=jnp.float32, precision=EXACT
    )

    def pod_copy(k):
        peer = lax.rem(h + k, shards)
        return pltpu.make_async_remote_copy(
            src_ref=pod_terms.at[pl.ds(pl.multiple_of(peer * 8, 8), 8), :],
            dst_ref=pod_in.at[k],
            send_sem=pod_send.at[k],
            recv_sem=pod_recv.at[k],
            device_id=(d, peer),
            device_id_type=MESH,
        )

    @pl.loop(1, shards)
    def _(k):
        pod_copy(k).start()

    rack_row[...] = jnp.dot(
        k_diag, totals[...], preferred_element_type=jnp.float32, precision=EXACT
    )
    copies = [
        small_copy(totals, far_totals, 2, (far_d, h)),
        small_copy(rack_row, rack_row_in, 3, (diag_d, h)),
        small_copy(totals, near_totals, 4, (near_d, h)),
    ]
    for copy in copies:
        copy.start()
    next_far(AHEAD + 1)

    near_copy.wait()
    k_near_half = k_near.astype(jnp.bfloat16)

    @pl.loop(0, PARTS)
    def _(c):
        cols = pl.ds(pl.multiple_of(c * width, width), width)
        host_out[:, cols] += jnp.dot(
            k_near_half, near[:, cols], preferred_element_type=jnp.float32
        )

    next_far(AHEAD + 2)
    pod_sum[...] = pod_terms[pl.ds(pl.multiple_of(h * 8, 8), 8), :]

    @pl.loop(1, shards)
    def _(k):
        pod_copy(k).wait()
        pod_sum[...] += pod_in[k]

    pod_copies = [
        small_copy(pod_sum, slab_pods.at[0], 5, (far_d, h)),
        small_copy(pod_sum, slab_pods.at[1], 6, (diag_d, h)),
        small_copy(pod_sum, slab_pods.at[2], 7, (near_d, h)),
    ]
    for copy in pod_copies:
        copy.start()

    host_row_copy.wait()
    k_far_half = k_far.astype(jnp.bfloat16)
    host_scale = 1.0 / (window * math.sqrt(day))

    def finish(c):
        cols = pl.ds(pl.multiple_of(c * width, width), width)
        far_copy(c).wait_recv()
        host_out[:, cols] = (
            host_out[:, cols]
            + jnp.dot(k_far_half, far[:, cols], preferred_element_type=jnp.float32)
            + host_row_in[pl.ds(c, 1), :]
        ) * host_scale

    @pl.loop(0, PARTS - 2)
    def _(c):
        finish(c)

    for copy in copies + pod_copies:
        copy.wait()

    def exact(a, b):
        return jnp.dot(a, b, preferred_element_type=jnp.float32, precision=EXACT)

    def exact_nt(a, b):
        return lax.dot_general(a, b, NT, preferred_element_type=jnp.float32, precision=EXACT)

    rack_scale = 1.0 / (window * math.sqrt(day * hosts / racks))
    rack_out[...] = (
        exact(k_own, totals[...])
        + exact(k_near, near_totals[...])
        + exact(k_far, far_totals[...])
        + rack_row_in[0:1, :]
    ) * rack_scale
    pod_scale = 1.0 / (window * math.sqrt(day * hosts / POD_DEV))
    pods = (
        exact_nt(pod_sum[...], k_own)
        + exact_nt(slab_pods[0], k_far)
        + exact_nt(slab_pods[1], coefficients(d, diag_d, rows, rows))
        + exact_nt(slab_pods[2], k_near)
    ) * pod_scale
    pod_out[...] = pods[:POD_DEV]

    @pl.loop(PARTS - 2, PARTS)
    def _(c):
        finish(c)

    for c in range(PARTS - AHEAD, PARTS):
        far_copy(c).wait_send()


def on_device(load, host_rack, rack_pod):
    rows, hosts = load.shape
    racks = rack_pod.shape[0]
    shards = lax.axis_size("hst")
    f32 = jnp.float32
    hbm = pl.BlockSpec(memory_space=pltpu.HBM)
    vmem = pl.BlockSpec(memory_space=pltpu.VMEM)
    shapes = (
        pltpu.VMEM((rows, hosts), f32),
        pltpu.VMEM((rows, racks), f32),
        pltpu.VMEM((POD_DEV, rows), f32),
    )
    placed = functools.partial(pltpu.with_memory_space_constraint, memory_space=pltpu.HBM)
    host, rack, pod = pl.pallas_call(
        functools.partial(kernel, shards),
        out_shape=shapes,
        in_specs=[hbm, hbm, hbm],
        out_specs=(vmem, vmem, vmem),
        scratch_shapes=[
            pltpu.VMEM((rows, hosts), load.dtype),
            pltpu.VMEM((rows, hosts), load.dtype),
            pltpu.VMEM((rows, hosts), load.dtype),
            pltpu.VMEM((hosts // 128, 128), jnp.int32),
            pltpu.VMEM((racks // 128, 128), jnp.int32),
            pltpu.VMEM((hosts // 128, 128), jnp.int32),
            pltpu.VMEM((rows, 2 * racks), f32),
            pltpu.VMEM((rows, racks), f32),
            pltpu.VMEM((rows, racks), f32),
            pltpu.VMEM((rows, racks), f32),
            pltpu.VMEM((rows, racks), f32),
            pltpu.VMEM((8 * shards, rows), f32),
            pltpu.VMEM((shards, 8, rows), f32),
            pltpu.VMEM((8, rows), f32),
            pltpu.VMEM((SLABS - 1, 8, rows), f32),
            pltpu.VMEM((8, racks), f32),
            pltpu.VMEM((8, racks), f32),
            pltpu.VMEM((PARTS, hosts // PARTS), f32),
            pltpu.VMEM((PARTS, hosts // PARTS), f32),
            pltpu.SemaphoreType.DMA((3,)),
            pltpu.SemaphoreType.DMA((2,)),
            pltpu.SemaphoreType.DMA((PARTS,)),
            pltpu.SemaphoreType.DMA((PARTS,)),
            pltpu.SemaphoreType.DMA((8,)),
            pltpu.SemaphoreType.DMA((8,)),
            pltpu.SemaphoreType.DMA((shards,)),
            pltpu.SemaphoreType.DMA((shards,)),
        ],
        compiler_params=pltpu.CompilerParams(
            collective_id=0, has_side_effects=True, vmem_limit_bytes=40 * 1024 * 1024
        ),
        cost_estimate=pl.CostEstimate(
            flops=2 * rows * hosts * (3 * rows + 2 * racks),
            bytes_accessed=rows * hosts * 10,
            transcendentals=0,
        ),
    )(
        placed(load),
        placed(host_rack.reshape(hosts // 128, 128)),
        placed(rack_pod.reshape(racks // 128, 128)),
    )
    return host, rack, pod.T


def solution(mesh):
    in_specs = (P("slab", "hst"), P("hst"), P("hst"))
    out_specs = (P("slab", "hst"), P("slab", "hst"), P("slab", "hst"))
    return jax.shard_map(
        on_device, mesh=mesh, in_specs=in_specs, out_specs=out_specs, check_vma=False
    )
```

profile of v0, /device:TPU:0, one launch (start us, length us, event | category | flops | bytes accessed | tf_op | source)
XLA Modules:
  0.0 40.7 jit_solution(3655257613450604244)
XLA Ops:
  0.6 37.5 %shard_map.58 = (f32[72,8192]{1,0:T(8,128)S(1)}, f32[72,256]{1,0:T(8,128)S(1)}, f32[2,72]{1,0:T(2,128)S(1)}) custom-call(bf16[72,8192]{1,0:T(8,128)(2,1)} %load_hbm.1, s32[64,128]{1,0:T(8,128)} %bitcast.4, s32[2,128]{1,0:T(2,128)} %bitcast.5), custom_call_target="tpu_custom_call" | custom-call | flops 858783744 | bytes 5898240 | tf_op jit(solution)/shard_map/pallas_call | solution.py:313
  38.1 1.4 %copy.9 = f32[72,8192]{1,0:T(8,128)} copy(f32[72,8192]{1,0:T(8,128)S(1)} %get-tuple-element.9) | data formatting | bytes 4718592
  39.5 0.6 %copy.11 = f32[72,2]{0,1:T(2,128)} copy(f32[72,2]{0,1:T(2,128)S(1)} %bitcast.3) | data formatting | bytes 1152
  40.1 0.6 %copy.10 = f32[72,256]{1,0:T(8,128)} copy(f32[72,256]{1,0:T(8,128)S(1)} %get-tuple-element.10) | data formatting | bytes 147456
where the time goes:
time: 40.8 us; the launch traced here: 40.7 us
  Pallas kernels  37.5 us (92%)
  local copies, waits for them, and re-layouts  2.6 us (6%)
  between operations  0.64 us (2%)
    pallas_call x1, Pallas kernels, on_device(): pl.pallas_call(functools.partial(kernel, shards), out_shape=shapes, in_sp...  37.5 us
    unnamed x3, local copies, waits for them, and re-layouts  2.6 us

commit v1 on v0

--- a/solution.py
+++ b/solution.py
@@ -12,7 +12,7 @@
 POD_DEV = 2
 SLABS = 4
 PARTS = 8
-AHEAD = 5
+AHEAD = 2
 MESH = pl.DeviceIdType.MESH
 EXACT = lax.Precision.HIGHEST
 NT = (((1,), (1,)), ((), ()))
@@ -141,8 +141,7 @@
     partial[...] = jnp.zeros_like(partial)
     rack_ids = lax.broadcasted_iota(jnp.int32, (2 * racks, 128), 0)
 
-    @pl.loop(0, PARTS)
-    def _(c):
+    def add_members(c):
         cols = pl.ds(pl.multiple_of(c * width, width), width)
         member = jnp.concatenate(
             [
@@ -157,11 +156,15 @@
             own[:, cols], member, NT, preferred_element_type=jnp.float32
         )
 
+    pl.loop(0, PARTS // 2)(add_members)
+    next_far(2)
+    pl.loop(PARTS // 2, PARTS)(add_members)
+
     spill_copy = small_copy(
         partial.at[:, pl.ds(racks, racks)], spill, 0, (d, lax.rem(h + 1, shards))
     )
     spill_copy.start()
-    next_far(AHEAD)
+    next_far(3)
 
     k_own = coefficients(d, d, rows, rows)
     k_near = coefficients(d, near_d, rows, rows)
@@ -219,7 +222,7 @@
     ]
     for copy in copies:
         copy.start()
-    next_far(AHEAD + 1)
+    next_far(4)
 
     near_copy.wait()
     k_near_half = k_near.astype(jnp.bfloat16)
@@ -231,7 +234,6 @@
             k_near_half, near[:, cols], preferred_element_type=jnp.float32
         )
 
-    next_far(AHEAD + 2)
     pod_sum[...] = pod_terms[pl.ds(pl.multiple_of(h * 8, 8), 8), :]
 
     @pl.loop(1, shards)
@@ -246,6 +248,7 @@
     ]
     for copy in pod_copies:
         copy.start()
+    next_far(5)
 
     host_row_copy.wait()
     k_far_half = k_far.astype(jnp.bfloat16)
@@ -260,9 +263,10 @@
             + host_row_in[pl.ds(c, 1), :]
         ) * host_scale
 
-    @pl.loop(0, PARTS - 2)
-    def _(c):
+    pl.loop(0, PARTS - 4)(finish)
+    for c in range(PARTS - 4, PARTS - 2):
         finish(c)
+        next_far(c + 2)
 
     for copy in copies + pod_copies:
         copy.wait()
@@ -289,10 +293,7 @@
     ) * pod_scale
     pod_out[...] = pods[:POD_DEV]
 
-    @pl.loop(PARTS - 2, PARTS)
-    def _(c):
-        finish(c)
-
+    pl.loop(PARTS - 2, PARTS)(finish)
     for c in range(PARTS - AHEAD, PARTS):
         far_copy(c).wait_send()
 

time: 40.8 us -> 39.9 us (0.978)
  Pallas kernels: 37.5 us -> 36.5 us
    pallas_call x1, Pallas kernels: 37.5 us -> 36.5 us  [on_device(): pl.pallas_call(functools.partial(kernel, shards), out_shape=shapes, in_sp...]
where the time goes in v1:
time: 39.9 us; the launch traced here: 39.8 us
  Pallas kernels  36.5 us (91%)
  local copies, waits for them, and re-layouts  2.6 us (7%)
  between operations  0.64 us (2%)
    pallas_call x1, Pallas kernels, on_device(): pl.pallas_call(functools.partial(kernel, shards), out_shape=shapes, in_sp...  36.5 us
    unnamed x3, local copies, waits for them, and re-layouts  2.6 us

profile of v1, /device:TPU:0, one launch (start us, length us, event | category | flops | bytes accessed | tf_op | source)
XLA Modules:
  0.0 39.8 jit_solution(17261407738847277242)
XLA Ops:
  0.6 36.5 %shard_map.58 = (f32[72,8192]{1,0:T(8,128)S(1)}, f32[72,256]{1,0:T(8,128)S(1)}, f32[2,72]{1,0:T(2,128)S(1)}) custom-call(bf16[72,8192]{1,0:T(8,128)(2,1)} %load_hbm.1, s32[64,128]{1,0:T(8,128)} %bitcast.4, s32[2,128]{1,0:T(2,128)} %bitcast.5), custom_call_target="tpu_custom_call" | custom-call | flops 858783744 | bytes 5898240 | tf_op jit(solution)/shard_map/pallas_call | solution.py:314
  37.2 1.4 %copy.9 = f32[72,8192]{1,0:T(8,128)} copy(f32[72,8192]{1,0:T(8,128)S(1)} %get-tuple-element.9) | data formatting | bytes 4718592
  38.6 0.6 %copy.11 = f32[72,2]{0,1:T(2,128)} copy(f32[72,2]{0,1:T(2,128)S(1)} %bitcast.3) | data formatting | bytes 1152
  39.1 0.6 %copy.10 = f32[72,256]{1,0:T(8,128)} copy(f32[72,256]{1,0:T(8,128)S(1)} %get-tuple-element.10) | data formatting | bytes 147456
